TPU v7x, 32 devices: a whole 2x2x4 slice. The times are simulated.
32 devices in a mesh: nodes: 32 (over z, y, x, core).
Axes of the slice: x: 2, y: 2, z: 4, core: 2. Of those that a mesh axis runs over, the one named last changes fastest.
Arguments:
- features: bfloat16 [262144, 256], P('nodes'), may hold values from -6 to 6
- cluster_ids: int32 [262144], P('nodes'), may hold values from 0 to 16383, as said below
- tile_cols: int32 [128, 6], P('nodes'), may hold values from 0 to 127, as said below
- tile_counts: int32 [128], P('nodes'), may hold values from 1 to 6
- adjacency: bfloat16 [128, 6, 128, 128], P('nodes'), may hold values from -0.5 to 0.5
- w_first: bfloat16 [256, 256], replicated, may hold values from -0.375 to 0.375
- w_second: bfloat16 [256, 256], replicated, may hold values from -0.375 to 0.375
Outputs:
- unpooled: bfloat16 [262144, 256], P('nodes')
Inputs may be any that keep to these rules, and one draw needn't show every extreme that they name: `cluster_ids`: cluster c is held by device c // 512. Exactly 256 fine nodes of each device name clusters of other devices; at most 16 of them name clusters of any one other device, among at most 4 distinct clusters of it. `tile_cols`: tile s holds clusters s * 128 to s * 128 + 127; the column tiles named for a tile row of device p are tiles of devices p - 1, p and p + 1.
All inputs are finite; a program needn't handle non-finite values.
Results may differ from a plain program's by a relative error of at most 0.0051.
Values may be sent and summed in bfloat16 or wider, within the bound.
A program may use at most 64 MiB of HBM per device.

v0:
```python
import jax
import jax.numpy as jnp
from jax import lax
from jax.sharding import PartitionSpec as P

CL_DEV = 512
CAP = 16


def with_halo(block, sides, width):
    for axis, dim in sides:
        count = lax.axis_size(axis)
        forward = [(i, i + 1) for i in range(count - 1)]
        backward = [(target, source) for source, target in forward]
        low = lax.ppermute(
            lax.slice_in_dim(block, block.shape[dim] - width, None, axis=dim), axis, forward
        )
        high = lax.ppermute(lax.slice_in_dim(block, 0, width, axis=dim), axis, backward)
        block = jnp.concatenate([low, block, high], axis=dim)
    return block


def convolve(values, tile_cols, tile_counts, adjacency, myself):
    window = with_halo(values, (("nodes", 0),), values.shape[0])
    tile_size = adjacency.shape[2]
    per_device = tile_cols.shape[0]
    window_tiles = window.reshape(-1, tile_size, window.shape[1])
    offsets = tile_cols - (myself - 1) * per_device
    picked = window_tiles[offsets]
    live = jnp.arange(tile_cols.shape[1], dtype=jnp.int32)[None, :] < tile_counts[:, None]
    weights = jnp.where(live[:, :, None, None], adjacency, jnp.zeros((), adjacency.dtype))
    result = jnp.einsum("tkij,tkjf->tif", weights, picked, preferred_element_type=jnp.float32)
    return result.reshape(values.shape[0], values.shape[1])


def ranks_within(hot_table, lower_tri):
    running = jnp.dot(lower_tri, hot_table.astype(jnp.bfloat16), preferred_element_type=jnp.float32)
    return (jnp.sum(running * hot_table.astype(jnp.float32), axis=1) - 1.0).astype(jnp.int32)


def local(features, cluster_ids, tile_cols, tile_counts, adjacency, w_first, w_second):
    device_count = lax.axis_size("nodes")
    myself = lax.axis_index("nodes")
    fine_rows, width = features.shape
    clusters_here = CL_DEV
    local_ids = cluster_ids - myself * clusters_here
    owners = cluster_ids // clusters_here
    remote = owners != myself
    columns = jnp.arange(clusters_here, dtype=jnp.int32)
    block_rows = min(fine_rows, 2048)
    block_count = fine_rows // block_rows
    feature_blocks = features.reshape(block_count, block_rows, width)
    id_blocks = local_ids.reshape(block_count, block_rows)
    contract_rows = (((0,), (0,)), ((), ()))

    def pool_block(running, pieces):
        sums_acc, counts_acc = running
        rows_x, ids_x = pieces
        one_hot = ids_x[:, None] == columns[None, :]
        sums_acc = sums_acc + lax.dot_general(
            one_hot.astype(jnp.bfloat16), rows_x, contract_rows, preferred_element_type=jnp.float32
        )
        counts_acc = counts_acc + jnp.sum(one_hot.astype(jnp.float32), axis=0)
        return ((sums_acc, counts_acc), None)

    start = (
        jnp.zeros((clusters_here, width), jnp.float32),
        jnp.zeros((clusters_here,), jnp.float32),
    )
    (sums_all, counts_all), _ = lax.scan(pool_block, start, (feature_blocks, id_blocks))
    bound_count = device_count * CAP // 2
    chosen = jnp.nonzero(remote, size=bound_count, fill_value=0)[0].astype(jnp.int32)
    bound_rows = features[chosen]
    bound_global = cluster_ids[chosen]
    bound_owner = owners[chosen]
    bound_local = bound_global - bound_owner * clusters_here
    peers = jnp.arange(device_count, dtype=jnp.int32)
    owner_hot = (bound_owner[:, None] == peers[None, :]).astype(jnp.int32)
    bound_index = jnp.arange(bound_count, dtype=jnp.int32)
    lower_tri = (bound_index[:, None] >= bound_index[None, :]).astype(jnp.bfloat16)
    rank_in = ranks_within(owner_hot, lower_tri)
    slots = bound_owner * CAP + rank_in
    slot_range = jnp.arange(device_count * CAP, dtype=jnp.int32)
    slot_hot = slots[:, None] == slot_range[None, :]
    send_rows = lax.dot_general(
        slot_hot.astype(jnp.bfloat16), bound_rows, contract_rows, preferred_element_type=jnp.float32
    ).astype(jnp.bfloat16)
    send_ids = jnp.max(jnp.where(slot_hot, bound_local[:, None], -1), axis=0)
    got_rows, got_ids = (
        lax.all_to_all(
            send_rows.reshape(device_count, CAP, width),
            "nodes",
            split_axis=0,
            concat_axis=0,
            tiled=True,
        ),
        lax.all_to_all(
            send_ids.reshape(device_count, CAP), "nodes", split_axis=0, concat_axis=0, tiled=True
        ),
    )
    flat_ids = got_ids.reshape(-1)
    one_hot = flat_ids[:, None] == columns[None, :]
    sums_all = sums_all + lax.dot_general(
        one_hot.astype(jnp.bfloat16),
        got_rows.reshape(-1, width),
        contract_rows,
        preferred_element_type=jnp.float32,
    )
    counts_all = counts_all + jnp.sum(one_hot.astype(jnp.float32), axis=0)
    pooled = (sums_all / jnp.sqrt(counts_all + 1.0)[:, None]).astype(jnp.bfloat16)
    first_proj = jnp.dot(pooled, w_first, preferred_element_type=jnp.float32).astype(jnp.bfloat16)
    hidden = jnp.maximum(
        convolve(first_proj, tile_cols, tile_counts, adjacency, myself), 0.0
    ).astype(jnp.bfloat16)
    second_proj = jnp.dot(hidden, w_second, preferred_element_type=jnp.float32).astype(jnp.bfloat16)
    coarse = convolve(second_proj, tile_cols, tile_counts, adjacency, myself).astype(jnp.bfloat16)
    answer_hot = (flat_ids[:, None] == columns[None, :]).astype(jnp.bfloat16)
    answers = jnp.dot(answer_hot, coarse, preferred_element_type=jnp.float32).astype(jnp.bfloat16)
    returned = lax.all_to_all(
        answers.reshape(device_count, CAP, width), "nodes", split_axis=0, concat_axis=0, tiled=True
    )
    remote_part = jnp.dot(
        slot_hot.astype(jnp.bfloat16),
        returned.reshape(-1, width),
        preferred_element_type=jnp.float32,
    ).astype(jnp.bfloat16)
    block_starts = jnp.arange(block_count, dtype=jnp.int32) * block_rows
    row_range = jnp.arange(block_rows, dtype=jnp.int32)

    def unpool_block(unused, pieces):
        rows_x, ids_x, first_row = pieces
        one_hot = (ids_x[:, None] == columns[None, :]).astype(jnp.bfloat16)
        hit = ((first_row + row_range)[:, None] == chosen[None, :]).astype(jnp.bfloat16)
        value = (
            rows_x.astype(jnp.float32)
            + jnp.dot(one_hot, coarse, preferred_element_type=jnp.float32)
            + jnp.dot(hit, remote_part, preferred_element_type=jnp.float32)
        )
        return (unused, value.astype(jnp.bfloat16))

    _, result = lax.scan(
        unpool_block, jnp.zeros((), jnp.int32), (feature_blocks, id_blocks, block_starts)
    )
    return result.reshape(fine_rows, width)


def solution(mesh):
    placed = (
        P("nodes", None),
        P("nodes"),
        P("nodes", None),
        P("nodes"),
        P("nodes", None, None, None),
        P(),
        P(),
    )
    return jax.shard_map(
        local, mesh=mesh, in_specs=placed, out_specs=P("nodes", None), check_vma=False
    )
```

profile of v0, /device:TPU:0, one launch (start us, length us, event | category | flops | bytes accessed | tf_op | source)
XLA Modules:
  0.0 170.9 jit_solution(17864218267897688846)
XLA Ops:
  0.0 1.5 convert_reduce_fusion.1
  2.2 57.0 %scatter_custom_fusion = s32[256]{0:T(256)S(1)} fusion(s32[8192]{0:T(1024)S(1)} %bitcast.86, s32[8192]{0:T(1024)S(1)} %ne.56, s32[]{:T(128)} %copy.29), kind=kCustom, calls=%fused_computation.103 | custom fusion | flops 8192 | bytes 1028 | tf_op jit(solution)/shard_map/scatter-add | solution.py:72
  59.7 0.7 compare_select_fusion.8
  61.1 2.0 %gather_fusion.1 = s32[256]{0:T(256)S(1)} fusion(s32[8192]{0:T(1024)} %param.12, s32[1024]{0:T(1024)S(1)} %pad_clamp_fusion.1), kind=kCustom, calls=%fused_computation.1 | custom fusion | bytes 3072 | tf_op jit(solution)/shard_map/gather | solution.py:74
  63.1 1.7 %gather_fusion = s32[256]{0:T(256)S(1)} fusion(s32[8192]{0:T(1024)S(1)} %get-tuple-element.162, s32[1024]{0:T(1024)S(1)} %pad_clamp_fusion.1), kind=kCustom, calls=%fused_computation | custom fusion | bytes 3072 | tf_op jit(solution)/shard_map/gather | solution.py:75
  65.9 7.3 %all-to-all-start = ((s32[32,1,16]{2,1,0:T(1,128)}), s32[32,1,16]{2,1,0:T(1,128)S(1)}, u32[]{:S(2)}, u32[]{:S(2)}) async-start(s32[32,1,16]{2,1,0:T(1,128)} %bitcast.7), calls=%async_computation | async-start | bytes 32768 | tf_op jit(solution)/shard_map/all_to_all | solution.py:97
  73.3 3.7 %gather_fusion.2 = bf16[256,256]{1,0:T(8,128)(2,1)S(1)} fusion(bf16[8192,256]{1,0:T(8,128)(2,1)} %param.11, s32[1024]{0:T(1024)S(1)} %pad_clamp_fusion.1), kind=kCustom, calls=%fused_computation.2 | custom fusion | bytes 263168 | tf_op jit(solution)/shard_map/gather | solution.py:73
  77.0 14.3 %while.25 = (s32[]{:T(128)}, f32[512,256]{1,0:T(8,128)S(1)}, f32[512]{0:T(512)S(1)}, s32[4,2048]{1,0:T(4,128)S(1)}, bf16[4,2048,256]{2,1,0:T(8,128)(2,1)}, /*index=5*/s32[]{:T(128)}, s32[]{:T(128)}) while((s32[]{:T(128)}, f32[512,256]{1,0:T(8,128)S(1)}, f32[512]{0:T(512)S(1)}, s32[4,2048]{1,0:T(4,128)S(1)}, ...), condition=%wide.region_8.9_spmd.clone, body=%wide.region_6.8_spmd.clone.sunk | while | flops 541327872 | bytes 2138716 | solution.py:70
  77.0 2.9 %fusion.73 = f32[512,256]{1,0:T(8,128)S(1)} fusion(s32[2048]{0:T(1024)S(1)} %bitcast.82, bf16[4,2048,256]{2,1,0:T(8,128)(2,1)} %get-tuple-element.264, s32[]{:T(128)} %get-tuple-element.253, f32[512,256]{1,0:T(8,128)S(1)} %get-tuple-element.254, pred[]{:T(512)S(6)} %compare.15), kind=kOutput, calls=%fused_computation.28.clone.1 | convolution fusion | flops 538181632 | bytes 2105857 | tf_op jit(solution)/shard_map/while/body/eval_jaxpr/dot_general | solution.py:60
  80.6 2.9 %fusion.73 = f32[512,256]{1,0:T(8,128)S(1)} fusion(s32[2048]{0:T(1024)S(1)} %bitcast.82, bf16[4,2048,256]{2,1,0:T(8,128)(2,1)} %get-tuple-element.264, s32[]{:T(128)} %get-tuple-element.253, f32[512,256]{1,0:T(8,128)S(1)} %get-tuple-element.254, pred[]{:T(512)S(6)} %compare.15), kind=kOutput, calls=%fused_computation.28.clone.1 | convolution fusion | flops 538181632 | bytes 2105857 | tf_op jit(solution)/shard_map/while/body/eval_jaxpr/dot_general | solution.py:60
  84.1 2.9 %fusion.73 = f32[512,256]{1,0:T(8,128)S(1)} fusion(s32[2048]{0:T(1024)S(1)} %bitcast.82, bf16[4,2048,256]{2,1,0:T(8,128)(2,1)} %get-tuple-element.264, s32[]{:T(128)} %get-tuple-element.253, f32[512,256]{1,0:T(8,128)S(1)} %get-tuple-element.254, pred[]{:T(512)S(6)} %compare.15), kind=kOutput, calls=%fused_computation.28.clone.1 | convolution fusion | flops 538181632 | bytes 2105857 | tf_op jit(solution)/shard_map/while/body/eval_jaxpr/dot_general | solution.py:60
  87.7 2.9 %fusion.73 = f32[512,256]{1,0:T(8,128)S(1)} fusion(s32[2048]{0:T(1024)S(1)} %bitcast.82, bf16[4,2048,256]{2,1,0:T(8,128)(2,1)} %get-tuple-element.264, s32[]{:T(128)} %get-tuple-element.253, f32[512,256]{1,0:T(8,128)S(1)} %get-tuple-element.254, pred[]{:T(512)S(6)} %compare.15), kind=kOutput, calls=%fused_computation.28.clone.1 | convolution fusion | flops 538181632 | bytes 2105857 | tf_op jit(solution)/shard_map/while/body/eval_jaxpr/dot_general | solution.py:60
  91.2 1.1 convolution_convert_fusion.3
  92.4 5.8 %all-to-all-start.1 = ((bf16[32,16,256]{2,1,0:T(8,128)(2,1)}), bf16[32,16,256]{2,1,0:T(8,128)(2,1)S(1)}, u32[]{:S(2)}, u32[]{:S(2)}) async-start(bf16[32,16,256]{2,1,0:T(8,128)(2,1)} %bitcast.8), calls=%async_computation.1 | async-start | bytes 524288 | tf_op jit(solution)/shard_map/all_to_all | solution.py:90
  98.9 0.7 reduce.7
  99.9 8.9 %all-to-all-done.1 = bf16[32,16,256]{2,1,0:T(8,128)(2,1)S(1)} async-done(((bf16[32,16,256]{2,1,0:T(8,128)(2,1)}), bf16[32,16,256]{2,1,0:T(8,128)(2,1)S(1)}, u32[]{:S(2)}, u32[]{:S(2)}) %all-to-all-start.1) | async-done | bytes 262176 | tf_op jit(solution)/shard_map/all_to_all | solution.py:90
  108.8 0.7 convolution_convert_fusion.2
  109.5 1.8 %collective-permute-start = (bf16[512,256]{1,0:T(8,128)(2,1)S(1)}, bf16[512,256]{1,0:T(8,128)(2,1)S(1)}, u32[]{:S(2)}, u32[]{:S(2)}) collective-permute-start(bf16[512,256]{1,0:T(8,128)(2,1)S(1)} %convolution_convert_fusion.2), channel_id=1, source_target_pairs={{0,1},{1,2},{2,3},{3,4},{4,5},{5,6},{6,7},{7,8},{8,9},{9,10},{10,1... | collective-permute-start | bytes 786440 | tf_op jit(solution)/shard_map/ppermute | solution.py:15
  111.4 1.3 collective-permute-start.1
  112.8 2.0 %collective-permute-done.1 = bf16[512,256]{1,0:T(8,128)(2,1)S(1)} collective-permute-done((bf16[512,256]{1,0:T(8,128)(2,1)S(1)}, bf16[512,256]{1,0:T(8,128)(2,1)S(1)}, u32[]{:S(2)}, u32[]{:S(2)}) %collective-permute-start.1) | collective-permute-done | bytes 262176 | tf_op jit(solution)/shard_map/ppermute | solution.py:18
  116.6 7.3 %collective-permute-start.2 = (bf16[512,256]{1,0:T(8,128)(2,1)S(1)}, bf16[512,256]{1,0:T(8,128)(2,1)S(1)}, u32[]{:S(2)}, u32[]{:S(2)}) collective-permute-start(bf16[512,256]{1,0:T(8,128)(2,1)S(1)} %convolution_convert_fusion.1), channel_id=1, source_target_pairs={{0,1},{1,2},{2,3},{3,4},{4,5},{5,6},{6,7},{7,8},{8,9},{9,10},{10,1... | collective-permute-start | bytes 786440 | tf_op jit(solution)/shard_map/ppermute | solution.py:15
  123.9 1.3 collective-permute-start.3
  125.3 2.1 %collective-permute-done.3 = bf16[512,256]{1,0:T(8,128)(2,1)S(1)} collective-permute-done((bf16[512,256]{1,0:T(8,128)(2,1)S(1)}, bf16[512,256]{1,0:T(8,128)(2,1)S(1)}, u32[]{:S(2)}, u32[]{:S(2)}) %collective-permute-start.3) | collective-permute-done | bytes 262176 | tf_op jit(solution)/shard_map/ppermute | solution.py:18
  128.5 1.1 convolution_convert_fusion
  129.6 10.6 %all-to-all-start.2 = ((bf16[32,16,256]{2,1,0:T(8,128)(2,1)}), bf16[32,16,256]{2,1,0:T(8,128)(2,1)S(1)}, u32[]{:S(2)}, u32[]{:S(2)}) async-start(bf16[32,16,256]{2,1,0:T(8,128)(2,1)} %bitcast.21), calls=%async_computation.2 | async-start | bytes 524288 | tf_op jit(solution)/shard_map/all_to_all | solution.py:119
  140.2 10.6 %all-to-all-done.2 = bf16[32,16,256]{2,1,0:T(8,128)(2,1)S(1)} async-done(((bf16[32,16,256]{2,1,0:T(8,128)(2,1)}), bf16[32,16,256]{2,1,0:T(8,128)(2,1)S(1)}, u32[]{:S(2)}, u32[]{:S(2)}) %all-to-all-start.2) | async-done | bytes 262176 | tf_op jit(solution)/shard_map/all_to_all | solution.py:119
  151.1 19.8 %while.24 = (s32[]{:T(128)}, bf16[4,2048,256]{2,1,0:T(8,128)(2,1)}, bf16[4,2048,256]{2,1,0:T(8,128)(2,1)}, s32[4,2048]{1,0:T(4,128)S(1)}, bf16[512,256]{1,0:T(8,...) while((s32[]{:T(128)}, bf16[4,2048,256]{2,1,0:T(8,128)(2,1)}, ...), condition=%wide.region_13.14_spmd.clone, body=%wide.region_12.13_spmd.clone.sunk | while | flops 808978432 | bytes 6727281 | solution.py:141
  151.7 0.7 iota_add_fusion.2
  153.0 3.1 %fusion.71 = bf16[4,2048,256]{2,1,0:T(8,128)(2,1)} fusion(bf16[4,2048,256]{2,1,0:T(8,128)(2,1)} %get-tuple-element.277, s32[]{:T(128)} %get-tuple-element.276, f32[2048,256]{1,0:T(8,128)S(1)} %fusion.70, bf16[512,256]{1,0:T(8,128)(2,1)S(1)} %get-tuple-element.289, s32[2048]{0:T(1024)S(1)} %bitcast.84, bf16[4,2048,256]{2,1,0:T(8,128)(2,1)} %get-tuple-element.287), kind=kOutput, calls=%fused_computation.15.clone.1 | convolution fusion | flops 540016640 | bytes 4465152 | tf_op jit(solution)/shard_map/while/body/eval_jaxpr/dot_general | solution.py:136
  157.9 3.1 %fusion.71 = bf16[4,2048,256]{2,1,0:T(8,128)(2,1)} fusion(bf16[4,2048,256]{2,1,0:T(8,128)(2,1)} %get-tuple-element.277, s32[]{:T(128)} %get-tuple-element.276, f32[2048,256]{1,0:T(8,128)S(1)} %fusion.70, bf16[512,256]{1,0:T(8,128)(2,1)S(1)} %get-tuple-element.289, s32[2048]{0:T(1024)S(1)} %bitcast.84, bf16[4,2048,256]{2,1,0:T(8,128)(2,1)} %get-tuple-element.287), kind=kOutput, calls=%fused_computation.15.clone.1 | convolution fusion | flops 540016640 | bytes 4465152 | tf_op jit(solution)/shard_map/while/body/eval_jaxpr/dot_general | solution.py:136
  162.8 3.1 %fusion.71 = bf16[4,2048,256]{2,1,0:T(8,128)(2,1)} fusion(bf16[4,2048,256]{2,1,0:T(8,128)(2,1)} %get-tuple-element.277, s32[]{:T(128)} %get-tuple-element.276, f32[2048,256]{1,0:T(8,128)S(1)} %fusion.70, bf16[512,256]{1,0:T(8,128)(2,1)S(1)} %get-tuple-element.289, s32[2048]{0:T(1024)S(1)} %bitcast.84, bf16[4,2048,256]{2,1,0:T(8,128)(2,1)} %get-tuple-element.287), kind=kOutput, calls=%fused_computation.15.clone.1 | convolution fusion | flops 540016640 | bytes 4465152 | tf_op jit(solution)/shard_map/while/body/eval_jaxpr/dot_general | solution.py:136
  167.8 3.1 %fusion.71 = bf16[4,2048,256]{2,1,0:T(8,128)(2,1)} fusion(bf16[4,2048,256]{2,1,0:T(8,128)(2,1)} %get-tuple-element.277, s32[]{:T(128)} %get-tuple-element.276, f32[2048,256]{1,0:T(8,128)S(1)} %fusion.70, bf16[512,256]{1,0:T(8,128)(2,1)S(1)} %get-tuple-element.289, s32[2048]{0:T(1024)S(1)} %bitcast.84, bf16[4,2048,256]{2,1,0:T(8,128)(2,1)} %get-tuple-element.287), kind=kOutput, calls=%fused_computation.15.clone.1 | convolution fusion | flops 540016640 | bytes 4465152 | tf_op jit(solution)/shard_map/while/body/eval_jaxpr/dot_general | solution.py:136
  (79 shorter events, 16.4 us)
Async XLA Ops:
  0.0 108.8 %copy-start = (bf16[256,256]{1,0:T(8,128)(2,1)S(1)}, bf16[256,256]{1,0:T(8,128)(2,1)}, u32[]{:S(2)}) copy-start(bf16[256,256]{1,0:T(8,128)(2,1)} %param.16) | copy-start | bytes 393220
  65.9 26.5 %all-to-all-start = ((s32[32,1,16]{2,1,0:T(1,128)}), s32[32,1,16]{2,1,0:T(1,128)S(1)}, u32[]{:S(2)}, u32[]{:S(2)}) async-start(s32[32,1,16]{2,1,0:T(1,128)} %bitcast.7), calls=%async_computation | async-start | bytes 32768 | tf_op jit(solution)/shard_map/all_to_all | solution.py:97
  77.0 21.3 %copy-start.2 = (s32[4,6]{1,0:T(4,128)S(1)}, s32[4,6]{1,0:T(4,128)}, u32[]{:S(2)}) copy-start(s32[4,6]{1,0:T(4,128)} %param.13) | copy-start | bytes 292
  91.2 21.4 %copy-start.4 = (s32[4]{0:T(128)S(1)}, s32[4]{0:T(128)}, u32[]{:S(2)}) copy-start(s32[4]{0:T(128)} %param.14) | copy-start | bytes 52
  92.4 16.4 %all-to-all-start.1 = ((bf16[32,16,256]{2,1,0:T(8,128)(2,1)}), bf16[32,16,256]{2,1,0:T(8,128)(2,1)S(1)}, u32[]{:S(2)}, u32[]{:S(2)}) async-start(bf16[32,16,256]{2,1,0:T(8,128)(2,1)} %bitcast.8), calls=%async_computation.1 | async-start | bytes 524288 | tf_op jit(solution)/shard_map/all_to_all | solution.py:90
  109.5 3.2 %collective-permute-start = (bf16[512,256]{1,0:T(8,128)(2,1)S(1)}, bf16[512,256]{1,0:T(8,128)(2,1)S(1)}, u32[]{:S(2)}, u32[]{:S(2)}) collective-permute-start(bf16[512,256]{1,0:T(8,128)(2,1)S(1)} %convolution_convert_fusion.2), channel_id=1, source_target_pairs={{0,1},{1,2},{2,3},{3,4},{4,5},{5,6},{6,7},{7,8},{8,9},{9,10},{10,1... | collective-permute-start | bytes 786440 | tf_op jit(solution)/shard_map/ppermute | solution.py:15
  111.4 3.4 %collective-permute-start.1 = (bf16[512,256]{1,0:T(8,128)(2,1)S(1)}, bf16[512,256]{1,0:T(8,128)(2,1)S(1)}, u32[]{:S(2)}, u32[]{:S(2)}) collective-permute-start(bf16[512,256]{1,0:T(8,128)(2,1)S(1)} %convolution_convert_fusion.2), channel_id=1, source_target_pairs={{1,0},{2,1},{3,2},{4,3},{5,4},{6,5},{7,6},{8,7},{9,8},{10,9},{11,1... | collective-permute-start | bytes 786440 | tf_op jit(solution)/shard_map/ppermute | solution.py:18
  112.8 2.8 %copy-start.3 = (bf16[4,6,128,128]{3,2,1,0:T(8,128)(2,1)S(1)}, bf16[4,6,128,128]{3,2,1,0:T(8,128)(2,1)}, u32[]{:S(2)}) copy-start(bf16[4,6,128,128]{3,2,1,0:T(8,128)(2,1)} %param.15) | copy-start | bytes 2359300
  115.5 0.9 copy-start.1
  116.6 8.6 %collective-permute-start.2 = (bf16[512,256]{1,0:T(8,128)(2,1)S(1)}, bf16[512,256]{1,0:T(8,128)(2,1)S(1)}, u32[]{:S(2)}, u32[]{:S(2)}) collective-permute-start(bf16[512,256]{1,0:T(8,128)(2,1)S(1)} %convolution_convert_fusion.1), channel_id=1, source_target_pairs={{0,1},{1,2},{2,3},{3,4},{4,5},{5,6},{6,7},{7,8},{8,9},{9,10},{10,1... | collective-permute-start | bytes 786440 | tf_op jit(solution)/shard_map/ppermute | solution.py:15
  123.9 3.4 %collective-permute-start.3 = (bf16[512,256]{1,0:T(8,128)(2,1)S(1)}, bf16[512,256]{1,0:T(8,128)(2,1)S(1)}, u32[]{:S(2)}, u32[]{:S(2)}) collective-permute-start(bf16[512,256]{1,0:T(8,128)(2,1)S(1)} %convolution_convert_fusion.1), channel_id=1, source_target_pairs={{1,0},{2,1},{3,2},{4,3},{5,4},{6,5},{7,6},{8,7},{9,8},{10,9},{11,1... | collective-permute-start | bytes 786440 | tf_op jit(solution)/shard_map/ppermute | solution.py:18
  129.6 21.2 %all-to-all-start.2 = ((bf16[32,16,256]{2,1,0:T(8,128)(2,1)}), bf16[32,16,256]{2,1,0:T(8,128)(2,1)S(1)}, u32[]{:S(2)}, u32[]{:S(2)}) async-start(bf16[32,16,256]{2,1,0:T(8,128)(2,1)} %bitcast.21), calls=%async_computation.2 | async-start | bytes 524288 | tf_op jit(solution)/shard_map/all_to_all | solution.py:119
where the time goes:
time: 172 us; the launch traced here: 171 us
  other arithmetic  67.1 us (39%)
  starting transfers between devices  35.4 us (21%)
  matrix products  30.4 us (18%)
  waiting for transfers between devices  23.6 us (14%)
  local copies, waits for them, and re-layouts  13.8 us (8%)
    scatter-add x1, other arithmetic, local(): jnp.nonzero(remote, size=bound_count, fill_value=0)[0].astype(jnp.int32)  57 us
    dot_general x4, matrix products, unpool_block(): jnp.dot(one_hot, coarse, preferred_element_type=jnp.float32)  12.3 us
    dot_general x4, matrix products, pool_block(): lax.dot_general(one_hot.astype(jnp.bfloat16), rows_x, contract_rows, pref...  11.7 us
    all_to_all x1, starting transfers between devices, local(): lax.all_to_all(answers.reshape(device_count, CAP, width), 'nodes', split_...  10.6 us
    all_to_all x1, waiting for transfers between devices, local(): lax.all_to_all(answers.reshape(device_count, CAP, width), 'nodes', split_...  10.6 us
    ppermute x2, starting transfers between devices, with_halo(): lax.ppermute(lax.slice_in_dim(block, block.shape[dim] - width, None, axis...  9.13 us
    all_to_all x1, waiting for transfers between devices, local(): lax.all_to_all(send_rows.reshape(device_count, CAP, width), 'nodes', spli...  8.88 us
    all_to_all x1, starting transfers between devices, local(): lax.all_to_all(send_ids.reshape(device_count, CAP), 'nodes', split_axis=0...  7.3 us
  transfers between devices with their start and end apart: 7, of which 4 were waited for; matrix products, arithmetic and copies ran while one was open for 12% of the time, Pallas kernels for 0%

commit v1 on v0

v1 whole, which is shorter than its diff:
```python
import functools

import jax
import jax.numpy as jnp
from jax import lax
from jax.experimental import pallas as pl
from jax.experimental.pallas import tpu as pltpu
from jax.sharding import PartitionSpec as P

CL_DEV = 512
DCAP = 4
LANES = 128
MSG = 16
ROWS = 8
F32 = jnp.float32
BF16 = jnp.bfloat16
I32 = jnp.int32
MESH = pl.DeviceIdType.MESH
CONTRACT_LANES = (((1,), (1,)), ((), ()))
CONTRACT_ROWS = (((0,), (0,)), ((), ()))


def dot(a, b, dims=None):
    if dims is None:
        return jnp.dot(a, b, preferred_element_type=F32)
    return lax.dot_general(a, b, dims, preferred_element_type=F32)


def iota(shape, axis):
    return lax.broadcasted_iota(I32, shape, axis)


def ones_where(mask):
    return jnp.where(mask, jnp.float32(1), jnp.float32(0)).astype(BF16)


def hot_of_rows(keys, ids):
    return jnp.concatenate(
        [ones_where(keys == ids[r : r + 1, :]) for r in range(ids.shape[0])], axis=1
    )


def place(rows, slots, part, group):
    row = iota((rows, slots), 0)
    slot = iota((rows, slots), 1)
    at = (slot // DCAP) * group + part * DCAP + slot % DCAP
    return ones_where(row == at)


def take(rows, slots, part, group):
    slot = iota((slots, rows), 0)
    row = iota((slots, rows), 1)
    at = (slot // DCAP) * group + part * DCAP + slot % DCAP
    return ones_where(row == at)


def find_slots(counts, me):
    high = counts.shape[0]
    per = CL_DEV // LANES
    slots = high // per * DCAP
    row = iota((high, LANES), 0)
    present = jnp.logical_and(counts > 0.5, row // per != me)
    hot = ones_where(present)
    before = ones_where(iota((LANES, LANES), 0) < iota((LANES, LANES), 1))
    ones = jnp.ones((LANES, LANES), BF16)
    row_total = dot(hot, ones).astype(BF16)
    r0, r1 = iota((high, high), 0), iota((high, high), 1)
    earlier = ones_where(jnp.logical_and(r0 // per == r1 // per, r1 < r0))
    rank = dot(hot, before) + dot(earlier, row_total)
    lows = iota((LANES, LANES), 0).astype(F32).astype(BF16)
    s0, h1 = iota((slots, high), 0), iota((slots, high), 1)
    low = jnp.zeros((slots, LANES), F32)
    top = jnp.zeros((slots, LANES), F32)
    number = jnp.zeros((slots, LANES), F32)
    for r in range(DCAP):
        mine = jnp.logical_and(present, jnp.abs(rank - r) < 0.5)
        chosen = ones_where(mine)
        weighed = jnp.where(mine, counts, 0.0).astype(BF16)
        pick = jnp.logical_and(s0 % DCAP == r, s0 // DCAP == h1 // per)
        pick_one = ones_where(pick)
        pick_top = jnp.where(pick, h1 % per, 0).astype(F32).astype(BF16)
        flag = dot(chosen, ones).astype(BF16)
        low = low + dot(pick_one, dot(chosen, lows).astype(BF16))
        number = number + dot(pick_one, dot(weighed, ones).astype(BF16))
        top = top + dot(pick_top, flag)
    return low, top, number


def coarse_kernel(
    n, ids_ref, cols_ref, live_ref, feat_ref, adj_ref, w1_ref, w2_ref,
    table_ref, key_ref,
    fbuf, fsem, cnt_ref, acc_ref, sacc_ref, skey_ref, msg, rec, msg2, rec2, win1, win2,
    send1, recv1, send2, recv2, hsend, hrecv,
):
    me = lax.axis_index("nodes")
    fine, width = fbuf.shape
    chunk = ROWS * LANES
    chunks = fine // chunk
    tiles, kt = cols_ref.shape
    tile = adj_ref.shape[2]
    slots = n * DCAP
    per = CL_DEV // LANES
    high = n * per
    half = width // 2

    def load(c):
        at = pl.ds(c * chunk, chunk)
        return pltpu.make_async_copy(feat_ref.at[at], fbuf.at[at], fsem.at[c])

    for c in range(chunks):
        load(c).start()

    barrier = pltpu.get_barrier_semaphore()

    def greet(j, x):
        pl.semaphore_signal(barrier, inc=1, device_id=(lax.rem(me + j, n),), device_id_type=MESH)
        return x

    lax.fori_loop(1, n, greet, 0)

    cnt_ref[...] = jnp.zeros_like(cnt_ref)

    def count(c, x):
        ids = ids_ref[pl.ds(pl.multiple_of(c * ROWS, ROWS), ROWS), :]
        hi = hot_of_rows(iota((high, LANES), 0), ids // LANES)
        lo = hot_of_rows(iota((LANES, LANES), 0), ids % LANES)
        cnt_ref[...] += dot(hi, lo, CONTRACT_LANES)
        return x

    lax.fori_loop(0, chunks, count, 0)

    low, top, number = find_slots(cnt_ref[...], me)
    owner = iota((slots, LANES), 0) // DCAP
    key = (owner * CL_DEV).astype(F32) + top * LANES + low
    key = jnp.where(number > 0.5, key, -1.0).astype(I32)
    skey_ref[...] = key
    key_ref[...] = key.T[0:ROWS, :]

    for c in range(chunks):
        load(c).wait()

    sacc_ref[...] = jnp.zeros_like(sacc_ref)

    def pool_slots(c, x):
        ids = ids_ref[pl.ds(pl.multiple_of(c * ROWS, ROWS), ROWS), :]
        rows = fbuf[pl.ds(pl.multiple_of(c * chunk, chunk), chunk), :]
        sacc_ref[...] += dot(hot_of_rows(skey_ref[...], ids), rows)
        return x

    lax.fori_loop(0, chunks, pool_slots, 0)

    sums = sacc_ref[...].astype(BF16)
    parts = [sums[:, :half], sums[:, half:], low.astype(BF16), (number * 4.0 + top).astype(BF16)]
    packed = jnp.zeros((MSG * n, LANES), F32)
    for i, part in enumerate(parts):
        packed = packed + dot(place(MSG * n, slots, i, MSG), part)
    msg[...] = packed.astype(BF16)
    mine = pl.ds(pl.multiple_of(me * MSG, MSG), MSG)
    rec[mine, :] = jnp.zeros((MSG, LANES), BF16)
    rec2[mine, :] = jnp.zeros((MSG, LANES), BF16)
    pl.semaphore_wait(barrier, n - 1)

    def send(src, dst, ssem, rsem, peer):
        return pltpu.make_async_remote_copy(
            src_ref=src.at[pl.ds(pl.multiple_of(peer * MSG, MSG), MSG)],
            dst_ref=dst.at[mine],
            send_sem=ssem.at[peer],
            recv_sem=rsem.at[me],
            device_id=(peer,),
            device_id_type=MESH,
        )

    def arrived(src, dst, ssem, rsem, peer):
        at = pl.ds(pl.multiple_of(peer * MSG, MSG), MSG)
        return pltpu.make_async_remote_copy(
            src_ref=src.at[at],
            dst_ref=dst.at[at],
            send_sem=ssem.at[peer],
            recv_sem=rsem.at[peer],
            device_id=(peer,),
            device_id_type=MESH,
        )

    def exchange_start(*refs):
        def go(j, x):
            send(*refs, lax.rem(me + j, n)).start()
            return x

        lax.fori_loop(1, n, go, 0)

    def exchange_wait(*refs):
        def go(j, x):
            arrived(*refs, lax.rem(me + j, n)).wait_recv()
            return x

        lax.fori_loop(1, n, go, 0)

    def exchange_end(*refs):
        def go(j, x):
            arrived(*refs, lax.rem(me + j, n)).wait_send()
            return x

        lax.fori_loop(1, n, go, 0)

    first = (msg, rec, send1, recv1)
    second = (msg2, rec2, send2, recv2)
    exchange_start(*first)

    acc_ref[...] = jnp.zeros_like(acc_ref)

    def pool_own(c, x):
        ids = ids_ref[pl.ds(pl.multiple_of(c * ROWS, ROWS), ROWS), :] - me * CL_DEV
        rows = fbuf[pl.ds(pl.multiple_of(c * chunk, chunk), chunk), :]
        acc_ref[...] += dot(hot_of_rows(iota((CL_DEV, LANES), 0), ids), rows)
        return x

    lax.fori_loop(0, chunks, pool_own, 0)

    eye = iota((LANES, LANES), 0) == iota((LANES, LANES), 1)
    own_counts = jnp.concatenate(
        [
            jnp.sum(jnp.where(eye, cnt_ref[pl.ds(me * per + a, 1), :], 0.0), axis=1, keepdims=True)
            for a in range(per)
        ],
        axis=0,
    )

    exchange_wait(*first)
    got = rec[...]
    got_left, got_right, got_low, got_code = (
        dot(take(MSG * n, slots, i, MSG), got) for i in range(4)
    )
    got_code = got_code.astype(I32)
    got_number = got_code // 4
    got_id = (got_code % 4) * LANES + got_low.astype(I32)
    got_id = jnp.where(got_number > 0, got_id, -1)
    answer_hot = jnp.concatenate(
        [ones_where(got_id == iota((slots, LANES), 1) + a * LANES) for a in range(per)], axis=1
    )
    got_all = jnp.concatenate(
        [got_left.astype(BF16), got_right.astype(BF16), got_number.astype(F32).astype(BF16)], axis=1
    )
    more = dot(answer_hot, got_all, CONTRACT_ROWS)
    counts = own_counts + more[:, width : width + 1]
    pooled = ((acc_ref[...] + more[:, :width]) / jnp.sqrt(counts + 1.0)).astype(BF16)

    def halo(win, i):
        up = pltpu.make_async_remote_copy(
            src_ref=win.at[pl.ds(tiles, tiles)],
            dst_ref=win.at[pl.ds(0, tiles)],
            send_sem=hsend.at[i],
            recv_sem=hrecv.at[i],
            device_id=(lax.rem(me + 1, n),),
            device_id_type=MESH,
        )
        down = pltpu.make_async_remote_copy(
            src_ref=win.at[pl.ds(tiles, tiles)],
            dst_ref=win.at[pl.ds(2 * tiles, tiles)],
            send_sem=hsend.at[i + 1],
            recv_sem=hrecv.at[i + 1],
            device_id=(lax.rem(me + n - 1, n),),
            device_id_type=MESH,
        )
        return up, down

    def fill_halo(win, values, i):
        win[pl.ds(tiles, tiles), :, :] = values.reshape(tiles, tile, width)
        up, down = halo(win, i)
        low_end, high_end = me == 0, me == n - 1

        @pl.when(jnp.logical_not(high_end))
        def _():
            up.start()

        @pl.when(jnp.logical_not(low_end))
        def _():
            down.start()

        @pl.when(low_end)
        def _():
            win[pl.ds(0, tiles), :, :] = jnp.zeros((tiles, tile, width), BF16)

        @pl.when(high_end)
        def _():
            win[pl.ds(2 * tiles, tiles), :, :] = jnp.zeros((tiles, tile, width), BF16)

        @pl.when(jnp.logical_not(low_end))
        def _():
            up.wait_recv()
            down.wait_send()

        @pl.when(jnp.logical_not(high_end))
        def _():
            down.wait_recv()
            up.wait_send()

    def convolve(win):
        result = []
        for t in range(tiles):
            total = jnp.zeros((tile, width), F32)
            for k in range(kt):
                at = jnp.clip(cols_ref[t, k] - (me - 1) * tiles, 0, 3 * tiles - 1)
                keep = jnp.broadcast_to(k < live_ref[0, t], (tile, tile))
                weights = jnp.where(keep, adj_ref[t, k].astype(F32), 0.0).astype(BF16)
                total = total + dot(weights, win[at])
            result.append(total)
        return jnp.concatenate(result, axis=0)

    fill_halo(win1, dot(pooled, w1_ref[...]).astype(BF16), 0)
    hidden = jnp.maximum(convolve(win1), 0.0).astype(BF16)
    fill_halo(win2, dot(hidden, w2_ref[...]).astype(BF16), 2)
    coarse = convolve(win2).astype(BF16)
    answers = dot(answer_hot, coarse).astype(BF16)
    packed = dot(place(MSG * n, slots, 0, MSG), answers[:, :half])
    packed = packed + dot(place(MSG * n, slots, 1, MSG), answers[:, half:])
    msg2[...] = packed.astype(BF16)
    exchange_start(*second)
    table_ref[pl.ds(0, CL_DEV), :] = coarse
    exchange_end(*first)
    exchange_wait(*second)
    back = rec2[...]
    table_ref[pl.ds(CL_DEV, slots), :] = jnp.concatenate(
        [dot(take(MSG * n, slots, i, MSG), back) for i in range(2)], axis=1
    ).astype(BF16)
    exchange_end(*second)


def unpool_kernel(ids_ref, key_ref, table_ref, feat_ref, out_ref):
    me = lax.axis_index("nodes")
    own = me * CL_DEV
    own_keys = [iota((1, LANES), 1) + (own + a * LANES) for a in range(CL_DEV // LANES)]
    slots = key_ref.shape[1]
    table = table_ref[...]
    slot_keys = [key_ref[0:1, a * LANES : (a + 1) * LANES] for a in range(slots // LANES)]
    for r in range(ROWS):
        at = pl.ds(r * LANES, LANES)
        ids = jnp.broadcast_to(ids_ref[r : r + 1, :], (LANES, LANES)).T
        hot = jnp.concatenate([ones_where(ids == key) for key in own_keys + slot_keys], axis=1)
        value = feat_ref[at, :].astype(F32) + dot(hot, table)
        out_ref[at, :] = value.astype(BF16)


def local(features, cluster_ids, tile_cols, tile_counts, adjacency, w_first, w_second):
    n = lax.axis_size("nodes")
    fine, width = features.shape
    tiles, _ = tile_cols.shape
    tile = adjacency.shape[2]
    slots = n * DCAP
    high = n * (CL_DEV // LANES)
    chunk = ROWS * LANES
    chunks = fine // chunk
    ids = cluster_ids.reshape(fine // LANES, LANES)
    vmem = pl.BlockSpec(memory_space=pltpu.VMEM)
    smem = pl.BlockSpec(memory_space=pltpu.SMEM)
    hbm = pl.BlockSpec(memory_space=pl.ANY)
    dma = pltpu.SemaphoreType.DMA
    table, keys = pl.pallas_call(
        functools.partial(coarse_kernel, n),
        out_shape=(
            jax.ShapeDtypeStruct((CL_DEV + slots, width), BF16),
            jax.ShapeDtypeStruct((ROWS, slots), I32),
        ),
        in_specs=[vmem, smem, smem, hbm, vmem, vmem, vmem],
        out_specs=(vmem, vmem),
        scratch_shapes=[
            pltpu.VMEM((fine, width), BF16),
            dma((chunks,)),
            pltpu.VMEM((high, LANES), F32),
            pltpu.VMEM((CL_DEV, width), F32),
            pltpu.VMEM((slots, width), F32),
            pltpu.VMEM((slots, LANES), I32),
            pltpu.VMEM((MSG * n, LANES), BF16),
            pltpu.VMEM((MSG * n, LANES), BF16),
            pltpu.VMEM((MSG * n, LANES), BF16),
            pltpu.VMEM((MSG * n, LANES), BF16),
            pltpu.VMEM((3 * tiles, tile, width), BF16),
            pltpu.VMEM((3 * tiles, tile, width), BF16),
            dma((n,)),
            dma((n,)),
            dma((n,)),
            dma((n,)),
            dma((4,)),
            dma((4,)),
        ],
        compiler_params=pltpu.CompilerParams(
            collective_id=0, has_side_effects=True, vmem_limit_bytes=48 * 1024 * 1024
        ),
    )(ids, tile_cols, tile_counts.reshape(1, tiles), features, adjacency, w_first, w_second)
    return pl.pallas_call(
        unpool_kernel,
        grid=(chunks,),
        out_shape=jax.ShapeDtypeStruct((fine, width), BF16),
        in_specs=[
            pl.BlockSpec((ROWS, LANES), lambda i: (i, 0)),
            pl.BlockSpec((ROWS, slots), lambda i: (0, 0)),
            pl.BlockSpec((CL_DEV + slots, width), lambda i: (0, 0)),
            pl.BlockSpec((chunk, width), lambda i: (i, 0)),
        ],
        out_specs=pl.BlockSpec((chunk, width), lambda i: (i, 0)),
        compiler_params=pltpu.CompilerParams(vmem_limit_bytes=32 * 1024 * 1024),
    )(ids, keys, table, features)


def solution(mesh):
    placed = (
        P("nodes", None),
        P("nodes"),
        P("nodes", None),
        P("nodes"),
        P("nodes", None, None, None),
        P(),
        P(),
    )
    return jax.shard_map(
        local, mesh=mesh, in_specs=placed, out_specs=P("nodes", None), check_vma=False
    )
```

time: 172 us -> 53.3 us (0.31)
  other arithmetic: 67.1 us -> 0 us
  Pallas kernels: 0 us -> 45.7 us
  starting transfers between devices: 35.4 us -> 0 us
  matrix products: 30.4 us -> 0 us
  waiting for transfers between devices: 23.6 us -> 0 us
  local copies, waits for them, and re-layouts: 13.8 us -> 7.22 us
    scatter-add x1 -> x0, other arithmetic: 57 us -> none  [local(): jnp.nonzero(remote, size=bound_count, fill_value=0)[0].astype(jnp.int32)]
    pallas_call x0 -> x2, Pallas kernels: none -> 45.7 us  [the longest x1 39.3 us: local(): pl.pallas_call(functools.partial(coarse_kernel, n), out_shape=(jax.ShapeD...]
    dot_general x20 -> x0, matrix products: 30.4 us -> none  [the longest x4 12.3 us: unpool_block(): jnp.dot(one_hot, coarse, preferred_element_type=jnp.float32)]
    all_to_all x3 -> x0, starting transfers between devices: 23.7 us -> none  [the longest x1 10.6 us: local(): lax.all_to_all(answers.reshape(device_count, CAP, width), 'nodes', split_...]
    all_to_all x3 -> x0, waiting for transfers between devices: 19.5 us -> none  [the longest x1 10.6 us: local(): lax.all_to_all(answers.reshape(device_count, CAP, width), 'nodes', split_...]
    ppermute x4 -> x0, starting transfers between devices: 11.7 us -> none  [the longest x2 9.13 us: with_halo(): lax.ppermute(lax.slice_in_dim(block, block.shape[dim] - width, None, axis...]
    gather x5 -> x0, local copies, waits for them, and re-layouts: 8.71 us -> none  [the longest x1 3.7 us: local(): bound_rows = features[chosen]]
    unnamed x10 -> x14, local copies, waits for them, and re-layouts: 0.48 us -> 7.22 us
  transfers between devices with their start and end apart: 7 -> 0, of which waited for: 4 -> 0; matrix products, arithmetic and copies ran while one was open for 12% -> 0% of each run, Pallas kernels for 0% -> 0%
where the time goes in v1:
time: 53.3 us; the launch traced here: 52.9 us
  Pallas kernels  45.7 us (86%)
  local copies, waits for them, and re-layouts  7.22 us (14%)
    pallas_call x1, Pallas kernels, local(): pl.pallas_call(functools.partial(coarse_kernel, n), out_shape=(jax.ShapeD...  39.3 us
    unnamed x14, local copies, waits for them, and re-layouts  7.22 us
    pallas_call x1, Pallas kernels, local(): pl.pallas_call(unpool_kernel, grid=(chunks,), out_shape=jax.ShapeDtypeStr...  6.43 us

profile of v1, /device:TPU:0, one launch (start us, length us, event | category | flops | bytes accessed | tf_op | source)
XLA Modules:
  0.0 52.9 jit_solution(13226239585031019833)
XLA Ops:
  0.0 0.0 copy-start
  0.0 2.2 %copy-done = bf16[8192,256]{1,0:T(8,128)(2,1)S(1)} copy-done((bf16[8192,256]{1,0:T(8,128)(2,1)S(1)}, bf16[8192,256]{1,0:T(8,128)(2,1)}, u32[]{:S(2)}) %copy-start) | copy-done | bytes 4194328
  2.2 0.0 copy-start.1
  2.2 1.1 %copy-done.1 = bf16[4,6,128,128]{3,2,1,0:T(8,128)(2,1)S(1)} copy-done((bf16[4,6,128,128]{3,2,1,0:T(8,128)(2,1)S(1)}, bf16[4,6,128,128]{3,2,1,0:T(8,128)(2,1)}, u32[]{:S(2)}) %copy-start.1) | copy-done | bytes 786456
  3.3 0.0 copy-start.2
  3.3 0.8 %copy-done.2 = s32[8192]{0:T(1024)S(1)} copy-done((s32[8192]{0:T(1024)S(1)}, s32[8192]{0:T(1024)}, u32[]{:S(2)}) %copy-start.2) | copy-done | bytes 32792
  4.1 0.0 copy-start.3
  4.1 0.9 %copy-done.3 = bf16[256,256]{1,0:T(8,128)(2,1)S(1)} copy-done((bf16[256,256]{1,0:T(8,128)(2,1)S(1)}, bf16[256,256]{1,0:T(8,128)(2,1)}, u32[]{:S(2)}) %copy-start.3) | copy-done | bytes 131096
  5.0 0.0 copy-start.4
  5.0 0.9 %copy-done.4 = bf16[256,256]{1,0:T(8,128)(2,1)S(1)} copy-done((bf16[256,256]{1,0:T(8,128)(2,1)S(1)}, bf16[256,256]{1,0:T(8,128)(2,1)}, u32[]{:S(2)}) %copy-start.4) | copy-done | bytes 131096
  5.9 0.0 copy-start.5
  5.9 0.7 %copy-done.5 = s32[4,6]{1,0:T(4,128)S(1)} copy-done((s32[4,6]{1,0:T(4,128)S(1)}, s32[4,6]{1,0:T(4,128)}, u32[]{:S(2)}) %copy-start.5) | copy-done | bytes 120
  6.6 0.0 copy-start.6
  6.6 0.7 %copy-done.6 = s32[4]{0:T(128)S(1)} copy-done((s32[4]{0:T(128)S(1)}, s32[4]{0:T(128)}, u32[]{:S(2)}) %copy-start.6) | copy-done | bytes 40
  7.2 39.3 %shard_map.73 = (bf16[640,256]{1,0:T(8,128)(2,1)S(1)}, s32[8,128]{1,0:T(8,128)S(1)}) custom-call(s32[64,128]{1,0:T(8,128)S(1)} %bitcast.2, s32[4,6]{1,0:T(4,128)S(1)} %copy-done.5, s32[1,4]{1,0:T(1,128)S(1)} %bitcast.4, bf16[8192,256]{1,0:T(8,128)(2,1)S(1)} %copy-done, bf16[4,6,128,128]{3,2,1,0:T(8,128)(2,1)S(1)} %copy-done.1, ...), custom_call_target="tpu_custom_call" | custom-call | tf_op jit(solution)/shard_map/pallas_call | solution.py:357
  46.5 6.4 %shard_map.74 = bf16[8192,256]{1,0:T(8,128)(2,1)} custom-call(s32[64,128]{1,0:T(8,128)S(1)} %bitcast.3, s32[8,128]{1,0:T(8,128)S(1)} %get-tuple-element.7.key_ref, bf16[640,256]{1,0:T(8,128)(2,1)S(1)} %get-tuple-element.8.table_ref, bf16[8192,256]{1,0:T(8,128)(2,1)S(1)} %copy-done), custom_call_target="tpu_custom_call" | custom-call | tf_op jit(solution)/shard_map/pallas_call | solution.py:389
Async XLA Ops:
  0.0 2.2 %copy-start = (bf16[8192,256]{1,0:T(8,128)(2,1)S(1)}, bf16[8192,256]{1,0:T(8,128)(2,1)}, u32[]{:S(2)}) copy-start(bf16[8192,256]{1,0:T(8,128)(2,1)} %feat_ref.3) | copy-start | bytes 12582916
  2.2 1.1 %copy-start.1 = (bf16[4,6,128,128]{3,2,1,0:T(8,128)(2,1)S(1)}, bf16[4,6,128,128]{3,2,1,0:T(8,128)(2,1)}, u32[]{:S(2)}) copy-start(bf16[4,6,128,128]{3,2,1,0:T(8,128)(2,1)} %adj_ref.1) | copy-start | bytes 2359300
  3.3 0.8 %copy-start.2 = (s32[8192]{0:T(1024)S(1)}, s32[8192]{0:T(1024)}, u32[]{:S(2)}) copy-start(s32[8192]{0:T(1024)} %param.8) | copy-start | bytes 98308
  4.1 0.9 %copy-start.3 = (bf16[256,256]{1,0:T(8,128)(2,1)S(1)}, bf16[256,256]{1,0:T(8,128)(2,1)}, u32[]{:S(2)}) copy-start(bf16[256,256]{1,0:T(8,128)(2,1)} %w1_ref.1) | copy-start | bytes 393220
  5.0 0.9 %copy-start.4 = (bf16[256,256]{1,0:T(8,128)(2,1)S(1)}, bf16[256,256]{1,0:T(8,128)(2,1)}, u32[]{:S(2)}) copy-start(bf16[256,256]{1,0:T(8,128)(2,1)} %w2_ref.1) | copy-start | bytes 393220
  5.9 0.7 %copy-start.5 = (s32[4,6]{1,0:T(4,128)S(1)}, s32[4,6]{1,0:T(4,128)}, u32[]{:S(2)}) copy-start(s32[4,6]{1,0:T(4,128)} %cols_ref.1) | copy-start | bytes 292
  6.6 0.7 %copy-start.6 = (s32[4]{0:T(128)S(1)}, s32[4]{0:T(128)}, u32[]{:S(2)}) copy-start(s32[4]{0:T(128)} %param.10) | copy-start | bytes 52

commit v2 on v1

--- a/solution.py
+++ b/solution.py
@@ -11,10 +11,16 @@
 DCAP = 4
 LANES = 128
 MSG = 16
+VMEM_BYTES = 63 * 1024 * 1024
+PACK = 16
+DSHIFT = 2
+LSHIFT = 7
+PSHIFT = 2
 ROWS = 8
 F32 = jnp.float32
 BF16 = jnp.bfloat16
 I32 = jnp.int32
+I16 = jnp.int16
 MESH = pl.DeviceIdType.MESH
 CONTRACT_LANES = (((1,), (1,)), ((), ()))
 CONTRACT_ROWS = (((0,), (0,)), ((), ()))
@@ -34,23 +40,33 @@
     return jnp.where(mask, jnp.float32(1), jnp.float32(0)).astype(BF16)
 
 
+def hot16(a, b):
+    return jnp.where(a == b, jnp.ones((), BF16), jnp.zeros((), BF16))
+
+
+def short_rows(row, count):
+    one = jnp.broadcast_to(row, (PACK, LANES)).astype(I16)
+    return jnp.concatenate([one] * (count // PACK), axis=0)
+
+
 def hot_of_rows(keys, ids):
     return jnp.concatenate(
-        [ones_where(keys == ids[r : r + 1, :]) for r in range(ids.shape[0])], axis=1
+        [hot16(keys, short_rows(ids[r : r + 1, :], keys.shape[0])) for r in range(ids.shape[0])],
+        axis=1,
     )
 
 
 def place(rows, slots, part, group):
     row = iota((rows, slots), 0)
     slot = iota((rows, slots), 1)
-    at = (slot // DCAP) * group + part * DCAP + slot % DCAP
+    at = (slot >> DSHIFT) * group + part * DCAP + (slot & (DCAP - 1))
     return ones_where(row == at)
 
 
 def take(rows, slots, part, group):
     slot = iota((slots, rows), 0)
     row = iota((slots, rows), 1)
-    at = (slot // DCAP) * group + part * DCAP + slot % DCAP
+    at = (slot >> DSHIFT) * group + part * DCAP + (slot & (DCAP - 1))
     return ones_where(row == at)
 
 
@@ -59,13 +75,13 @@
     per = CL_DEV // LANES
     slots = high // per * DCAP
     row = iota((high, LANES), 0)
-    present = jnp.logical_and(counts > 0.5, row // per != me)
+    present = jnp.logical_and(counts > 0.5, (row >> PSHIFT) != me)
     hot = ones_where(present)
     before = ones_where(iota((LANES, LANES), 0) < iota((LANES, LANES), 1))
     ones = jnp.ones((LANES, LANES), BF16)
     row_total = dot(hot, ones).astype(BF16)
     r0, r1 = iota((high, high), 0), iota((high, high), 1)
-    earlier = ones_where(jnp.logical_and(r0 // per == r1 // per, r1 < r0))
+    earlier = ones_where(jnp.logical_and((r0 >> PSHIFT) == (r1 >> PSHIFT), r1 < r0))
     rank = dot(hot, before) + dot(earlier, row_total)
     lows = iota((LANES, LANES), 0).astype(F32).astype(BF16)
     s0, h1 = iota((slots, high), 0), iota((slots, high), 1)
@@ -76,9 +92,9 @@
         mine = jnp.logical_and(present, jnp.abs(rank - r) < 0.5)
         chosen = ones_where(mine)
         weighed = jnp.where(mine, counts, 0.0).astype(BF16)
-        pick = jnp.logical_and(s0 % DCAP == r, s0 // DCAP == h1 // per)
+        pick = jnp.logical_and((s0 & (DCAP - 1)) == r, (s0 >> DSHIFT) == (h1 >> PSHIFT))
         pick_one = ones_where(pick)
-        pick_top = jnp.where(pick, h1 % per, 0).astype(F32).astype(BF16)
+        pick_top = jnp.where(pick, h1 & (per - 1), 0).astype(F32).astype(BF16)
         flag = dot(chosen, ones).astype(BF16)
         low = low + dot(pick_one, dot(chosen, lows).astype(BF16))
         number = number + dot(pick_one, dot(weighed, ones).astype(BF16))
@@ -87,9 +103,9 @@
 
 
 def coarse_kernel(
-    n, ids_ref, cols_ref, live_ref, feat_ref, adj_ref, w1_ref, w2_ref,
+    n, ids_hbm, cols_hbm, live_hbm, feat_ref, adj_hbm, w1_hbm, w2_hbm,
     table_ref, key_ref,
-    fbuf, fsem, cnt_ref, acc_ref, sacc_ref, skey_ref, msg, rec, msg2, rec2, win1, win2,
+    ids_ref, cols_ref, live_ref, adj_ref, w1_ref, w2_ref, isem, fbuf, fsem, cnt_ref, acc_ref, sacc_ref, skey_ref, msg, rec, msg2, rec2, win1, win2,
     send1, recv1, send2, recv2, hsend, hrecv,
 ):
     me = lax.axis_index("nodes")
@@ -107,8 +123,16 @@
         at = pl.ds(c * chunk, chunk)
         return pltpu.make_async_copy(feat_ref.at[at], fbuf.at[at], fsem.at[c])
 
+    pairs = (
+        (ids_hbm, ids_ref), (cols_hbm, cols_ref), (live_hbm, live_ref),
+        (adj_hbm, adj_ref), (w1_hbm, w1_ref), (w2_hbm, w2_ref),
+    )
+    loads = [pltpu.make_async_copy(a, b, isem.at[i]) for i, (a, b) in enumerate(pairs)]
+    loads[0].start()
     for c in range(chunks):
         load(c).start()
+    for copy in loads[1:]:
+        copy.start()
 
     barrier = pltpu.get_barrier_semaphore()
 
@@ -122,18 +146,19 @@
 
     def count(c, x):
         ids = ids_ref[pl.ds(pl.multiple_of(c * ROWS, ROWS), ROWS), :]
-        hi = hot_of_rows(iota((high, LANES), 0), ids // LANES)
-        lo = hot_of_rows(iota((LANES, LANES), 0), ids % LANES)
+        hi = hot_of_rows(iota((high, LANES), 0).astype(I16), ids >> LSHIFT)
+        lo = hot_of_rows(iota((LANES, LANES), 0).astype(I16), ids & (LANES - 1))
         cnt_ref[...] += dot(hi, lo, CONTRACT_LANES)
         return x
 
+    loads[0].wait()
     lax.fori_loop(0, chunks, count, 0)
 
     low, top, number = find_slots(cnt_ref[...], me)
-    owner = iota((slots, LANES), 0) // DCAP
+    owner = iota((slots, LANES), 0) >> DSHIFT
     key = (owner * CL_DEV).astype(F32) + top * LANES + low
     key = jnp.where(number > 0.5, key, -1.0).astype(I32)
-    skey_ref[...] = key
+    skey_ref[...] = key.astype(I16)
     key_ref[...] = key.T[0:ROWS, :]
 
     for c in range(chunks):
@@ -211,11 +236,13 @@
     def pool_own(c, x):
         ids = ids_ref[pl.ds(pl.multiple_of(c * ROWS, ROWS), ROWS), :] - me * CL_DEV
         rows = fbuf[pl.ds(pl.multiple_of(c * chunk, chunk), chunk), :]
-        acc_ref[...] += dot(hot_of_rows(iota((CL_DEV, LANES), 0), ids), rows)
+        acc_ref[...] += dot(hot_of_rows(iota((CL_DEV, LANES), 0).astype(I16), ids), rows)
         return x
 
     lax.fori_loop(0, chunks, pool_own, 0)
 
+    for copy in loads[1:]:
+        copy.wait()
     eye = iota((LANES, LANES), 0) == iota((LANES, LANES), 1)
     own_counts = jnp.concatenate(
         [
@@ -231,8 +258,8 @@
         dot(take(MSG * n, slots, i, MSG), got) for i in range(4)
     )
     got_code = got_code.astype(I32)
-    got_number = got_code // 4
-    got_id = (got_code % 4) * LANES + got_low.astype(I32)
+    got_number = got_code >> 2
+    got_id = (got_code & 3) * LANES + got_low.astype(I32)
     got_id = jnp.where(got_number > 0, got_id, -1)
     answer_hot = jnp.concatenate(
         [ones_where(got_id == iota((slots, LANES), 1) + a * LANES) for a in range(per)], axis=1
@@ -242,7 +269,7 @@
     )
     more = dot(answer_hot, got_all, CONTRACT_ROWS)
     counts = own_counts + more[:, width : width + 1]
-    pooled = ((acc_ref[...] + more[:, :width]) / jnp.sqrt(counts + 1.0)).astype(BF16)
+    pooled = ((acc_ref[...] + more[:, :width]) * lax.rsqrt(counts + 1.0)).astype(BF16)
 
     def halo(win, i):
         up = pltpu.make_async_remote_copy(
@@ -332,10 +359,12 @@
     slots = key_ref.shape[1]
     table = table_ref[...]
     slot_keys = [key_ref[0:1, a * LANES : (a + 1) * LANES] for a in range(slots // LANES)]
+    keys = [short_rows(key, LANES) for key in own_keys + slot_keys]
     for r in range(ROWS):
         at = pl.ds(r * LANES, LANES)
         ids = jnp.broadcast_to(ids_ref[r : r + 1, :], (LANES, LANES)).T
-        hot = jnp.concatenate([ones_where(ids == key) for key in own_keys + slot_keys], axis=1)
+        ids = ids.astype(I16)
+        hot = jnp.concatenate([hot16(ids, key) for key in keys], axis=1)
         value = feat_ref[at, :].astype(F32) + dot(hot, table)
         out_ref[at, :] = value.astype(BF16)
 
@@ -351,8 +380,7 @@
     chunks = fine // chunk
     ids = cluster_ids.reshape(fine // LANES, LANES)
     vmem = pl.BlockSpec(memory_space=pltpu.VMEM)
-    smem = pl.BlockSpec(memory_space=pltpu.SMEM)
-    hbm = pl.BlockSpec(memory_space=pl.ANY)
+    hbm = pl.BlockSpec(memory_space=pltpu.HBM)
     dma = pltpu.SemaphoreType.DMA
     table, keys = pl.pallas_call(
         functools.partial(coarse_kernel, n),
@@ -360,15 +388,22 @@
             jax.ShapeDtypeStruct((CL_DEV + slots, width), BF16),
             jax.ShapeDtypeStruct((ROWS, slots), I32),
         ),
-        in_specs=[vmem, smem, smem, hbm, vmem, vmem, vmem],
+        in_specs=[hbm] * 7,
         out_specs=(vmem, vmem),
         scratch_shapes=[
+            pltpu.VMEM(ids.shape, I32),
+            pltpu.SMEM(tile_cols.shape, I32),
+            pltpu.SMEM((1, tiles), I32),
+            pltpu.VMEM(adjacency.shape, BF16),
+            pltpu.VMEM(w_first.shape, BF16),
+            pltpu.VMEM(w_second.shape, BF16),
+            dma((6,)),
             pltpu.VMEM((fine, width), BF16),
             dma((chunks,)),
             pltpu.VMEM((high, LANES), F32),
             pltpu.VMEM((CL_DEV, width), F32),
             pltpu.VMEM((slots, width), F32),
-            pltpu.VMEM((slots, LANES), I32),
+            pltpu.VMEM((slots, LANES), I16),
             pltpu.VMEM((MSG * n, LANES), BF16),
             pltpu.VMEM((MSG * n, LANES), BF16),
             pltpu.VMEM((MSG * n, LANES), BF16),
@@ -383,7 +418,7 @@
             dma((4,)),
         ],
         compiler_params=pltpu.CompilerParams(
-            collective_id=0, has_side_effects=True, vmem_limit_bytes=48 * 1024 * 1024
+            collective_id=0, has_side_effects=True, vmem_limit_bytes=VMEM_BYTES
         ),
     )(ids, tile_cols, tile_counts.reshape(1, tiles), features, adjacency, w_first, w_second)
     return pl.pallas_call(
@@ -397,7 +432,7 @@
             pl.BlockSpec((chunk, width), lambda i: (i, 0)),
         ],
         out_specs=pl.BlockSpec((chunk, width), lambda i: (i, 0)),
-        compiler_params=pltpu.CompilerParams(vmem_limit_bytes=32 * 1024 * 1024),
+        compiler_params=pltpu.CompilerParams(vmem_limit_bytes=VMEM_BYTES),
     )(ids, keys, table, features)
 
 

time: 53.3 us -> 48.4 us (0.908)
  local copies, waits for them, and re-layouts: 7.22 us -> 0 us
  Pallas kernels: 45.7 us -> 48.1 us
    unnamed x14 -> x0, local copies, waits for them, and re-layouts: 7.22 us -> none
    pallas_call x1, Pallas kernels: 6.43 us -> 8.99 us  [local(): pl.pallas_call(unpool_kernel, grid=(chunks,), out_shape=jax.ShapeDtypeStr...]
where the time goes in v2:
time: 48.4 us; the launch traced here: 48.1 us
  Pallas kernels  48.1 us (99%)
    pallas_call x1, Pallas kernels, local(): pl.pallas_call(functools.partial(coarse_kernel, n), out_shape=(jax.ShapeD...  39.1 us
    pallas_call x1, Pallas kernels, local(): pl.pallas_call(unpool_kernel, grid=(chunks,), out_shape=jax.ShapeDtypeStr...  8.99 us

profile of v2, /device:TPU:0, one launch (start us, length us, event | category | flops | bytes accessed | tf_op | source)
XLA Modules:
  0.0 48.1 jit_solution(3332944996961583192)
XLA Ops:
  0.0 39.1 %shard_map.73 = (bf16[640,256]{1,0:T(8,128)(2,1)}, s32[8,128]{1,0:T(8,128)}) custom-call(s32[64,128]{1,0:T(8,128)} %bitcast.2, s32[4,6]{1,0:T(4,128)} %cols_hbm.1, s32[1,4]{1,0:T(1,128)} %bitcast.4, bf16[8192,256]{1,0:T(8,128)(2,1)} %feat_ref.3, bf16[4,6,128,128]{3,2,1,0:T(8,128)(2,1)} %adj_hbm.1, bf16[256,256]{1,0:T(8,128)(2,1)} %w1_hbm.1, ...), custom_call_target="tpu_custom_call" | custom-call | tf_op jit(solution)/shard_map/pallas_call | solution.py:385
  39.1 9.0 %shard_map.74 = bf16[8192,256]{1,0:T(8,128)(2,1)} custom-call(s32[64,128]{1,0:T(8,128)} %bitcast.3, s32[8,128]{1,0:T(8,128)} %get-tuple-element.7.key_ref, bf16[640,256]{1,0:T(8,128)(2,1)} %get-tuple-element.8.table_ref, bf16[8192,256]{1,0:T(8,128)(2,1)} %feat_ref.3), custom_call_target="tpu_custom_call" | custom-call | tf_op jit(solution)/shard_map/pallas_call | solution.py:424

commit v3 on v2

--- a/solution.py
+++ b/solution.py
@@ -11,6 +11,7 @@
 DCAP = 4
 LANES = 128
 MSG = 16
+WIDE = 2
 VMEM_BYTES = 63 * 1024 * 1024
 PACK = 16
 DSHIFT = 2
@@ -360,7 +361,7 @@
     table = table_ref[...]
     slot_keys = [key_ref[0:1, a * LANES : (a + 1) * LANES] for a in range(slots // LANES)]
     keys = [short_rows(key, LANES) for key in own_keys + slot_keys]
-    for r in range(ROWS):
+    for r in range(ids_ref.shape[0]):
         at = pl.ds(r * LANES, LANES)
         ids = jnp.broadcast_to(ids_ref[r : r + 1, :], (LANES, LANES)).T
         ids = ids.astype(I16)
@@ -423,15 +424,15 @@
     )(ids, tile_cols, tile_counts.reshape(1, tiles), features, adjacency, w_first, w_second)
     return pl.pallas_call(
         unpool_kernel,
-        grid=(chunks,),
+        grid=(chunks // WIDE,),
         out_shape=jax.ShapeDtypeStruct((fine, width), BF16),
         in_specs=[
-            pl.BlockSpec((ROWS, LANES), lambda i: (i, 0)),
+            pl.BlockSpec((ROWS * WIDE, LANES), lambda i: (i, 0)),
             pl.BlockSpec((ROWS, slots), lambda i: (0, 0)),
             pl.BlockSpec((CL_DEV + slots, width), lambda i: (0, 0)),
-            pl.BlockSpec((chunk, width), lambda i: (i, 0)),
+            pl.BlockSpec((chunk * WIDE, width), lambda i: (i, 0)),
         ],
-        out_specs=pl.BlockSpec((chunk, width), lambda i: (i, 0)),
+        out_specs=pl.BlockSpec((chunk * WIDE, width), lambda i: (i, 0)),
         compiler_params=pltpu.CompilerParams(vmem_limit_bytes=VMEM_BYTES),
     )(ids, keys, table, features)
 

time: 48.4 us -> 46.5 us (0.961)
  Pallas kernels: 48.1 us -> 46.3 us
    pallas_call x1, Pallas kernels: 8.99 us -> 7.15 us  [local(): pl.pallas_call(unpool_kernel, grid=(chunks // WIDE,), out_shape=jax.Shape...]
where the time goes in v3:
time: 46.5 us; the launch traced here: 46.3 us
  Pallas kernels  46.3 us (100%)
    pallas_call x1, Pallas kernels, local(): pl.pallas_call(functools.partial(coarse_kernel, n), out_shape=(jax.ShapeD...  39.1 us
    pallas_call x1, Pallas kernels, local(): pl.pallas_call(unpool_kernel, grid=(chunks // WIDE,), out_shape=jax.Shape...  7.15 us

profile of v3, /device:TPU:0, one launch (start us, length us, event | category | flops | bytes accessed | tf_op | source)
XLA Modules:
  0.0 46.3 jit_solution(10823138325841655870)
XLA Ops:
  0.0 39.1 %shard_map.73 = (bf16[640,256]{1,0:T(8,128)(2,1)}, s32[8,128]{1,0:T(8,128)}) custom-call(s32[64,128]{1,0:T(8,128)} %bitcast.2, s32[4,6]{1,0:T(4,128)} %cols_hbm.1, s32[1,4]{1,0:T(1,128)} %bitcast.4, bf16[8192,256]{1,0:T(8,128)(2,1)} %feat_ref.3, bf16[4,6,128,128]{3,2,1,0:T(8,128)(2,1)} %adj_hbm.1, bf16[256,256]{1,0:T(8,128)(2,1)} %w1_hbm.1, ...), custom_call_target="tpu_custom_call" | custom-call | tf_op jit(solution)/shard_map/pallas_call | solution.py:386
  39.1 7.2 %shard_map.74 = bf16[8192,256]{1,0:T(8,128)(2,1)} custom-call(s32[64,128]{1,0:T(8,128)} %bitcast.3, s32[8,128]{1,0:T(8,128)} %get-tuple-element.7.key_ref, bf16[640,256]{1,0:T(8,128)(2,1)} %get-tuple-element.8.table_ref, bf16[8192,256]{1,0:T(8,128)(2,1)} %feat_ref.3), custom_call_target="tpu_custom_call" | custom-call | tf_op jit(solution)/shard_map/pallas_call | solution.py:425
